TPU v7x, 32 devices: a whole 2x2x4 slice. The times are simulated.
32 devices in a mesh: groups: 2 (over y), expert: 8 (over z, core), dp: 2 (over x).
Axes of the slice: x: 2, y: 2, z: 4, core: 2. Of those that a mesh axis runs over, the one named last changes fastest.
Arguments:
- tokens: bfloat16 [240, 2048], P(('groups', 'expert'), 'dp'), parts along dimension 0, may hold values from -6 to 6
- routes: int32 [240, 8], P(('groups', 'expert')), parts along dimension 0, may hold values from 0 to 15, all different within a row; in each aligned block of 15 rows (0 to 14, 15 to 29, ...) at most 11 rows name the same one
- route_weights: float32 [240, 8], P(('groups', 'expert')), parts along dimension 0, may hold values from 0.1 to 0.5
- w_gate: bfloat16 [16, 2048, 768], P('expert', 'dp'), may hold values from -0.125 to 0.125
- w_up: bfloat16 [16, 2048, 768], P('expert', 'dp'), may hold values from -0.125 to 0.125
- w_down: bfloat16 [16, 768, 2048], P('expert', None, 'dp'), may hold values from -0.21875 to 0.21875
- sae_encoder: bfloat16 [2048, 3072], P(None, ('expert', 'dp')), may hold values from -0.25 to 0.25
- enc_bias: float32 [3072], P(('expert', 'dp')), may hold values from -1 to 0.5
- sae_decoder: bfloat16 [3072, 2048], P(('expert', 'dp')), may hold values from -1 to 1
- dec_bias: float32 [2048], replicated, may hold values from -1.2 to 1.2
Outputs:
- moe_out: bfloat16 [240, 2048], P(('groups', 'expert'), 'dp'), parts along dimension 0
- grad_encoder: bfloat16 [4096, 3072], P('groups', ('expert', 'dp')), parts along dimension 0
- grad_decoder: bfloat16 [3072, 4096], P(('expert', 'dp'), 'groups'), parts along dimension 1
- grad_enc_bias: float32 [6144], P(('groups', 'expert', 'dp')), parts along dimension 0
- grad_dec_bias: float32 [4096], P('groups'), parts along dimension 0
- loss_mean: float32 [2], P('groups'), parts along dimension 0
There are 2 independent parts, one for each index of `groups`. A program takes and returns all parts, laid end to end along the dimension named above; an argument that names none is the same for every part. Nothing has to cross between parts.
Inputs may be any that keep to these rules, and one draw needn't show every extreme that they name: `routes`: in each aligned block of 15 rows (the rows of one index of the expert axis), no expert is named by more than 11 rows, and some block has an expert named by exactly 11 rows.
All inputs are finite; a program needn't handle non-finite values.
Results may differ from a plain program's by a relative error of at most 0.0085.
Values may be sent and summed in bfloat16 or wider, within the bound.
A program may use at most 64 MiB of HBM per device.

v0:
```python
import jax
import jax.numpy as jnp
from jax import lax
from jax.sharding import PartitionSpec as P

PENALTY = 0.5
SHARPNESS = 4.0
EPSILON = 1e-06


def gather_tokens(local_block):
    widened = lax.all_gather(local_block, "dp", axis=1, tiled=True)
    return lax.all_gather(widened, "expert", axis=0, tiled=True)


def local(
    tokens,
    routes,
    route_weights,
    w_gate,
    w_up,
    w_down,
    sae_encoder,
    enc_bias,
    sae_decoder,
    dec_bias,
):
    tok_count, top_count = routes.shape
    feature_width = tokens.shape[1]
    local_experts = w_gate.shape[0]
    peer_count = lax.axis_size("expert")
    total_experts = local_experts * peer_count
    capacity = min(tok_count, max(2, tok_count * top_count * 3 // (2 * total_experts)))
    flat_routes = routes.reshape(-1)
    expert_hot = (
        flat_routes[:, None] == jnp.arange(total_experts, dtype=jnp.int32)[None, :]
    ).astype(jnp.int32)
    earlier = jnp.cumsum(expert_hot, axis=0) - expert_hot
    position = jnp.sum(earlier * expert_hot, axis=1)
    slot_index = flat_routes * capacity + position
    slot_hot = slot_index[:, None] == jnp.arange(total_experts * capacity, dtype=jnp.int32)[None, :]
    slot_hot = slot_hot.reshape(tok_count, top_count, total_experts * capacity)
    dispatch_map = jnp.sum(slot_hot.astype(jnp.int32), axis=1).astype(jnp.bfloat16)
    combine_map = jnp.sum(slot_hot.astype(jnp.float32) * route_weights[:, :, None], axis=1)
    send_rows = lax.dot_general(
        dispatch_map, tokens, (((0,), (0,)), ((), ())), preferred_element_type=jnp.float32
    )
    send_blocks = send_rows.astype(jnp.bfloat16).reshape(
        peer_count, local_experts, capacity, feature_width
    )
    received = lax.all_to_all(send_blocks, "expert", split_axis=0, concat_axis=0, tiled=True)
    gate_part = jnp.einsum("secd,edf->secf", received, w_gate, preferred_element_type=jnp.float32)
    up_part = jnp.einsum("secd,edf->secf", received, w_up, preferred_element_type=jnp.float32)
    gate_full, up_full = lax.psum((gate_part, up_part), "dp")
    hidden = (jax.nn.silu(gate_full) * up_full).astype(jnp.bfloat16)
    outputs = jnp.einsum("secf,efd->secd", hidden, w_down, preferred_element_type=jnp.float32)
    returned = lax.all_to_all(
        outputs.astype(jnp.bfloat16), "expert", split_axis=0, concat_axis=0, tiled=True
    )
    returned_rows = returned.reshape(total_experts * capacity, feature_width).astype(jnp.float32)
    combined = jnp.dot(combine_map, returned_rows, precision=lax.Precision.HIGHEST)
    moe_out = combined.astype(jnp.bfloat16)
    all_tokens = gather_tokens(moe_out)
    centered = (all_tokens.astype(jnp.float32) - dec_bias).astype(jnp.bfloat16)
    pre_act = jnp.dot(centered, sae_encoder, preferred_element_type=jnp.float32) + enc_bias
    latent_codes = jax.nn.softplus(SHARPNESS * pre_act) / SHARPNESS
    codes_b = latent_codes.astype(jnp.bfloat16)
    decoder_wide = sae_decoder.astype(jnp.float32)
    dec_norm = jnp.sqrt(jnp.sum(decoder_wide * decoder_wide, axis=1) + EPSILON)
    partial_rows = lax.psum_scatter(
        jnp.dot(codes_b, sae_decoder, preferred_element_type=jnp.float32).astype(jnp.bfloat16),
        "expert",
        scatter_dimension=0,
        tiled=True,
    )
    recon_share = lax.psum_scatter(partial_rows, "dp", scatter_dimension=1, tiled=True).astype(
        jnp.float32
    )
    bias_share = lax.dynamic_slice_in_dim(
        dec_bias, lax.axis_index("dp") * feature_width, feature_width, 0
    )
    residual = recon_share + bias_share - moe_out.astype(jnp.float32)
    d_recon_share = (2.0 * residual).astype(jnp.bfloat16)
    d_recon = gather_tokens(d_recon_share)
    grad_codes = lax.dot_general(
        d_recon, sae_decoder, (((1,), (1,)), ((), ())), preferred_element_type=jnp.float32
    )
    d_pre = (grad_codes + PENALTY * dec_norm) * jax.nn.sigmoid(SHARPNESS * pre_act)
    d_pre_b = d_pre.astype(jnp.bfloat16)
    grad_encoder = lax.dot_general(
        centered, d_pre_b, (((0,), (0,)), ((), ())), preferred_element_type=jnp.float32
    )
    code_totals = jnp.sum(latent_codes, axis=0)
    grad_decoder = lax.dot_general(
        codes_b, d_recon, (((0,), (0,)), ((), ())), preferred_element_type=jnp.float32
    )
    grad_decoder = grad_decoder + PENALTY * code_totals[:, None] * decoder_wide / dec_norm[:, None]
    grad_enc_bias = jnp.sum(d_pre, axis=0)
    pre_totals = jnp.sum(d_pre_b.astype(jnp.float32), axis=0)
    bias_pull = jnp.dot(
        sae_encoder.astype(jnp.float32), pre_totals, precision=lax.Precision.HIGHEST
    )
    objective_part = jnp.sum(residual * residual) + PENALTY * jnp.sum(latent_codes * dec_norm)
    pull_total, objective = lax.psum((bias_pull, objective_part), ("expert", "dp"))
    grad_dec_bias = jnp.sum(d_recon.astype(jnp.float32), axis=0) - pull_total
    token_total = d_recon.shape[0]
    loss_mean = (objective / (token_total * d_recon.shape[1])).reshape(1)
    return (
        moe_out,
        grad_encoder.astype(jnp.bfloat16),
        grad_decoder.astype(jnp.bfloat16),
        grad_enc_bias,
        grad_dec_bias,
        loss_mean,
    )


def solution(mesh):
    in_specs = (
        P(("groups", "expert"), "dp"),
        P(("groups", "expert"), None),
        P(("groups", "expert"), None),
        P("expert", "dp", None),
        P("expert", "dp", None),
        P("expert", None, "dp"),
        P(None, ("expert", "dp")),
        P(("expert", "dp")),
        P(("expert", "dp"), None),
        P(),
    )
    out_specs = (
        P(("groups", "expert"), "dp"),
        P("groups", ("expert", "dp")),
        P(("expert", "dp"), "groups"),
        P(("groups", "expert", "dp")),
        P("groups"),
        P("groups"),
    )
    return jax.shard_map(local, mesh=mesh, in_specs=in_specs, out_specs=out_specs, check_vma=False)
```

profile of v0, /device:TPU:0, one launch (start us, length us, event | category | flops | bytes accessed | tf_op | source)
XLA Modules:
  0.0 243.7 jit_solution(8429499697273044430)
XLA Ops:
  7.2 0.0 copy-start
  7.2 0.0 all-reduce.6.cloned.1.call-start
  7.2 0.9 copy.33
  8.1 0.1 eq.29
  8.2 0.1 fusion.27
  8.3 0.2 reduce_window_sum.11
  8.5 0.2 select_reduce_fusion.1
  8.7 0.1 reduce_sum.93
  8.8 0.1 convert_reduce_fusion.1
  8.9 1.0 convolution_convert_fusion.2
  9.9 0.9 reshape.59
  10.9 1.6 copy.36
  12.5 18.0 %all_to_all.10 = bf16[8,2,11,1024]{3,1,2,0:T(2,128)(2,1)S(1)} all-to-all(bf16[8,2,11,1024]{3,1,2,0:T(2,128)(2,1)S(1)} %copy.36), channel_id=1, replica_groups=mesh['groups'=2,'expert'=8,'dp'=2] {'expert'}, dimensions={0} | all-to-all | bytes 720896 | tf_op jit(solution)/shard_map/all_to_all | solution.py:51
  30.4 3.4 %fusion.10 = f32[8,2,11,768]{3,2,0,1:T(8,128)} fusion(bf16[2,1024,768]{2,1,0:T(8,128)(2,1)} %param.13, bf16[8,2,11,1024]{3,1,2,0:T(2,128)(2,1)S(1)} %all_to_all.10), kind=kOutput, calls=%fused_computation.14 | convolution fusion | flops 276824064 | bytes 4046848 | tf_op jit(solution)/shard_map/secd,edf->secf/dot_general | solution.py:52
  33.8 0.0 copy-done.2
  33.8 1.5 fusion.13
  35.3 0.0 all-reduce.6.cloned.1.call-update
  35.4 50.7 %all-reduce.6.cloned.1.call-done = (f32[8,2,11,768]{3,2,0,1:T(8,128)}, f32[8,2,11,768]{3,2,0,1:T(8,128)}) async-done(((f32[8,2,11,768]{3,2,0,1:T(8,128)}, f32[8,2,11,768]{3,2,0,1:T(8,128)}), (f32[8,2,11,768]{3,2,0,1:T(8,128)}, f32[8,2,11,768]{3,2,0,1:T(8,128)})) %all-reduce.6.cloned.1.call-update) | async-done | bytes 1081360 | tf_op jit(solution)/shard_map/psum | solution.py:54
  86.1 0.0 copy-done
  86.1 2.0 fusion.19
  88.1 1.1 copy.39
  89.3 4.6 %all-to-all-start.1 = ((bf16[8,2,11,1024]{3,1,2,0:T(2,128)(2,1)}), bf16[8,2,11,1024]{3,1,2,0:T(2,128)(2,1)S(1)}, u32[]{:S(2)}, u32[]{:S(2)}) async-start(bf16[8,2,11,1024]{3,1,2,0:T(2,128)(2,1)} %copy.39), calls=%async_computation.1 | async-start | bytes 720896 | tf_op jit(solution)/shard_map/all_to_all | solution.py:57
  93.9 0.0 reduce-scatter.4.cloned.1.call-start
  93.9 0.0 copy-done.5
  93.9 0.1 copy.35
  94.0 0.1 select_reduce_fusion
  94.1 1.4 fusion.8
  95.5 0.6 broadcast_multiply_fusion
  96.1 9.6 %all-to-all-done.1 = bf16[8,2,11,1024]{3,1,2,0:T(2,128)(2,1)S(1)} async-done(((bf16[8,2,11,1024]{3,1,2,0:T(2,128)(2,1)}), bf16[8,2,11,1024]{3,1,2,0:T(2,128)(2,1)S(1)}, u32[]{:S(2)}, u32[]{:S(2)}) %all-to-all-start.1) | async-done | bytes 360480 | tf_op jit(solution)/shard_map/all_to_all | solution.py:57
  105.7 0.9 copy.40
  106.6 1.2 reshape.60
  107.8 0.3 convolution_convert_fusion.3
  108.1 0.0 copy-start.4
  108.1 0.0 copy-start.8
  108.1 4.7 %all_gather.12 = bf16[15,2048]{1,0:T(8,128)(2,1)S(1)} all-gather(bf16[15,1024]{1,0:T(8,128)(2,1)S(1)} %convolution_convert_fusion.3), channel_id=1, replica_groups=mesh['groups'=2,'expert'=8,'dp'=2] {'dp'}, dimensions={1}, use_global_device_ids=true | all-gather | bytes 92160 | tf_op jit(solution)/shard_map/all_gather | solution.py:12
  112.8 15.7 %all-gather = bf16[8,15,2048]{2,1,0:T(8,128)(2,1)} all-gather(bf16[1,15,2048]{2,1,0:T(8,128)(2,1)S(1)} %bitcast.49), channel_id=1, replica_groups=mesh['groups'=2,'expert'=8,'dp'=2] {'expert'}, dimensions={0}, use_global_device_ids=true | all-gather | bytes 552960 | tf_op jit(solution)/shard_map/all_gather | solution.py:13
  128.5 2.1 reshape.66
  130.7 2.6 %multiply_reduce_fusion = (f32[]{:T(128)}, f32[192]{0:T(256)S(1)}, f32[120,192]{0,1:T(8,128)S(1)}) fusion(f32[192]{0:T(256)} %get-tuple-element.16, f32[192]{0:T(256)} %param.17, bf16[2048,192]{0,1:T(8,128)(2,1)} %param.16, f32[120,2048]{1,0:T(8,128)} %reshape.66, f32[2048]{0:T(1024)} %param.19), kind=kOutput, calls=%fused_computation.34 | convolution fusion | flops 95139648 | bytes 1872132 | tf_op jit(solution)/shard_map/dot_general | solution.py:65
  133.3 2.3 convolution_convert_fusion.1
  135.6 19.6 %fusion = bf16[16,2048]{1,0:T(8,128)(2,1)S(1)} fusion(bf16[120,2048]{1,0:T(8,128)(2,1)} %convolution_convert_fusion.1), kind=kCustom, calls=%all-reduce-scatter | all-reduce-scatter fusion | flops 262145 | bytes 557568
  155.2 1.3 collective-permute-start
  156.5 0.0 copy-done.4
  156.5 0.0 copy-done.8
  156.6 0.6 dynamic-slice.4
  158.4 0.0 collective-permute-done
  158.5 0.2 concatenate
  158.7 0.7 constant_dynamic-slice_fusion
  159.3 0.0 reduce-scatter.4.cloned.1.call-update
  159.4 7.2 %reduce-scatter.4.cloned.1.call-done = bf16[15,1024]{1,0:T(8,128)(2,1)} async-done(((bf16[15,2048]{1,0:T(8,128)(2,1)}), bf16[15,1024]{1,0:T(8,128)(2,1)}) %reduce-scatter.4.cloned.1.call-update) | async-done | bytes 30736 | tf_op jit(solution)/shard_map/reduce_scatter | solution.py:76
  166.6 0.0 copy-done.3
  166.6 1.4 multiply_reduce_fusion.2
  168.0 4.6 %all_gather.14 = bf16[15,2048]{1,0:T(8,128)(2,1)S(1)} all-gather(bf16[15,1024]{1,0:T(8,128)(2,1)S(1)} %get-tuple-element.15), channel_id=1, replica_groups=mesh['groups'=2,'expert'=8,'dp'=2] {'dp'}, dimensions={1}, use_global_device_ids=true | all-gather | bytes 92160 | tf_op jit(solution)/shard_map/all_gather | solution.py:12
  172.6 15.9 %all-gather.1 = bf16[8,15,2048]{2,1,0:T(8,128)(2,1)} all-gather(bf16[1,15,2048]{2,1,0:T(8,128)(2,1)S(1)} %bitcast.48), channel_id=1, replica_groups=mesh['groups'=2,'expert'=8,'dp'=2] {'expert'}, dimensions={0}, use_global_device_ids=true | all-gather | bytes 552960 | tf_op jit(solution)/shard_map/all_gather | solution.py:13
  188.5 2.0 reshape.65
  190.5 1.2 convert_reduce_fusion
  191.7 0.0 copy-done.7
  191.7 2.4 convert_reduce_fusion.2
  194.0 1.5 fusion.33
  195.6 0.0 copy-done.1
  195.6 1.2 convolution_convert_fusion
  197.5 34.4 %all-reduce.2 = (f32[2048]{0:T(1024)S(1)}, f32[]{:T(128)}) all-reduce(f32[2048]{0:T(1024)S(1)} %bitcast.50, f32[]{:T(128)S(6)} %add.94), channel_id=1, replica_groups=mesh['groups'=2,'expert'=8,'dp'=2] {'expert','dp'}, use_global_device_ids=true, to_apply=%region_13.14 | all-reduce | flops 2049 | bytes 16392 | tf_op jit(solution)/shard_map/psum | solution.py:104
  231.9 0.6 sub.21
  233.1 0.0 copy-done.6
  233.1 2.6 %fusion.7 = bf16[192,2048]{1,0:T(8,128)(2,1)} fusion(bf16[120,2048]{1,0:T(8,128)(2,1)} %reshape.65, bf16[192,2048]{1,0:T(8,128)(2,1)} %param.18, f32[192]{0:T(256)S(1)} %copy-done.6, f32[192]{0:T(256)S(1)} %broadcast_multiply_fusion.1, f32[120,192]{0,1:T(8,128)S(1)} %get-tuple-element.19), kind=kOutput, calls=%fused_computation.7 | convolution fusion | flops 96522240 | bytes 2158080 | tf_op jit(solution)/shard_map/dot_general | solution.py:94
  (10 shorter events, 0.0 us)
Async XLA Ops:
  7.2 78.9 %copy-start = (bf16[2,768,1024]{2,1,0:T(8,128)(2,1)S(1)}, bf16[2,768,1024]{2,1,0:T(8,128)(2,1)}, u32[]{:S(2)}) copy-start(bf16[2,768,1024]{2,1,0:T(8,128)(2,1)} %param.15) | copy-start | bytes 9437188
  7.2 78.9 %all-reduce.6.cloned.1.call-start = ((), (), s32[]{:S(2)}) async-start(), calls=%async_computation.4 | async-start | bytes 3145728 | tf_op jit(solution)/shard_map/psum | solution.py:54
  10.9 23.0 %copy-start.2 = (bf16[2,1024,768]{2,1,0:T(8,128)(2,1)S(1)}, bf16[2,1024,768]{2,1,0:T(8,128)(2,1)}, u32[]{:S(2)}) copy-start(bf16[2,1024,768]{2,1,0:T(8,128)(2,1)} %param.14) | copy-start | bytes 9437188
  86.1 7.8 %copy-start.5 = (f32[15,8]{0,1:T(8,128)S(1)}, f32[15,8]{0,1:T(8,128)}, u32[]{:S(2)}) copy-start(f32[15,8]{0,1:T(8,128)} %param.12) | copy-start | bytes 1444
  89.3 16.5 %all-to-all-start.1 = ((bf16[8,2,11,1024]{3,1,2,0:T(2,128)(2,1)}), bf16[8,2,11,1024]{3,1,2,0:T(2,128)(2,1)S(1)}, u32[]{:S(2)}, u32[]{:S(2)}) async-start(bf16[8,2,11,1024]{3,1,2,0:T(2,128)(2,1)} %copy.39), calls=%async_computation.1 | async-start | bytes 720896 | tf_op jit(solution)/shard_map/all_to_all | solution.py:57
  93.9 72.7 %reduce-scatter.4.cloned.1.call-start = ((), (), s32[]{:S(2)}) async-start(), calls=%async_computation.3 | async-start | bytes 98304 | tf_op jit(solution)/shard_map/reduce_scatter | solution.py:76
  108.1 58.5 %copy-start.3 = (bf16[15,1024]{1,0:T(8,128)(2,1)}, bf16[15,1024]{1,0:T(8,128)(2,1)S(1)}, u32[]{:S(2)}) copy-start(bf16[15,1024]{1,0:T(8,128)(2,1)S(1)} %convolution_convert_fusion.3) | copy-start | bytes 92164
  108.1 48.4 %copy-start.4 = (f32[2048]{0:T(1024)S(1)}, f32[2048]{0:T(1024)}, u32[]{:S(2)}) copy-start(f32[2048]{0:T(1024)} %param.19) | copy-start | bytes 24580
  108.1 48.5 %copy-start.8 = (u32[32]{0:T(128)S(1)}, u32[32]{0:T(128)}, u32[]{:S(2)}) copy-start(u32[32]{0:T(128)} %constant.48) | copy-start | bytes 388
  130.7 61.0 %copy-start.7 = (f32[192]{0:T(256)S(1)}, f32[192]{0:T(256)}, u32[]{:S(2)}) copy-start(f32[192]{0:T(256)} %get-tuple-element.17) | copy-start | bytes 2308
  155.2 3.2 %collective-permute-start = (bf16[7,2048]{1,0:T(8,128)(2,1)S(1)}, bf16[7,2048]{1,0:T(8,128)(2,1)S(1)}, u32[]{:S(2)}, u32[]{:S(2)}) collective-permute-start(bf16[7,2048]{1,0:T(8,128)(2,1)S(1)} %slice), channel_id=1, source_target_pairs={{0,2},{2,4},{4,6},{6,8},{8,10},{10,12},{12,14},{1,3},{3,5},{5,7},{... | collective-permute-start | bytes 86024
  172.6 60.5 %copy-start.6 = (f32[192]{0:T(256)S(1)}, f32[192]{0:T(256)}, u32[]{:S(2)}) copy-start(f32[192]{0:T(256)} %get-tuple-element.18) | copy-start | bytes 2308
  190.5 5.1 %copy-start.1 = (f32[120,2048]{1,0:T(8,128)S(1)}, f32[120,2048]{1,0:T(8,128)}, u32[]{:S(2)}) copy-start(f32[120,2048]{1,0:T(8,128)} %reshape.66) | copy-start | bytes 2949124
Sparse Core Ops, SparseCore 0:
  35.5 50.5 all-reduce.5
  159.5 7.0 reduce-scatter.3
where the time goes:
time: 245 us; the launch traced here: 244 us
  blocking collectives  113 us (46%)
  waiting for transfers between devices  67.6 us (28%)
  matrix products  20.9 us (9%)
  between operations  18 us (7%)
  local copies, waits for them, and re-layouts  12.5 us (5%)
  starting transfers between devices  5.97 us (2%)
  other arithmetic  5.82 us (2%)
    psum x1, waiting for transfers between devices, local(): gate_full, up_full = lax.psum((gate_part, up_part), 'dp')  50.7 us
    psum x1, blocking collectives, local(): lax.psum((bias_pull, objective_part), ('expert', 'dp'))  34.4 us
    all_gather x2, blocking collectives, gather_tokens(): return lax.all_gather(widened, 'expert', axis=0, tiled=True)  31.6 us
    unnamed x1, blocking collectives  19.6 us
    all_to_all x1, blocking collectives, local(): lax.all_to_all(send_blocks, 'expert', split_axis=0, concat_axis=0, tiled=...  18 us
    all_to_all x1, waiting for transfers between devices, local(): lax.all_to_all(outputs.astype(jnp.bfloat16), 'expert', split_axis=0, conc...  9.63 us
    all_gather x2, blocking collectives, gather_tokens(): widened = lax.all_gather(local_block, 'dp', axis=1, tiled=True)  9.3 us
    reduce_scatter x1, waiting for transfers between devices, local(): lax.psum_scatter(partial_rows, 'dp', scatter_dimension=1, tiled=True)  7.24 us
  transfers between devices with their start and end apart: 4, of which 3 were waited for; matrix products, arithmetic and copies ran while one was open for 1% of the time, Pallas kernels for 0%

commit v1 on v0

--- a/solution.py
+++ b/solution.py
@@ -1,6 +1,10 @@
+import functools
+
 import jax
 import jax.numpy as jnp
 from jax import lax
+from jax.experimental import pallas as pl
+from jax.experimental.pallas import tpu as pltpu
 from jax.sharding import PartitionSpec as P
 
 PENALTY = 0.5
@@ -13,7 +17,7 @@
     return lax.all_gather(widened, "expert", axis=0, tiled=True)
 
 
-def local(
+def local_plain(
     tokens,
     routes,
     route_weights,
@@ -115,6 +119,454 @@
     )
 
 
+ROWS = 16
+NT = (((1,), (1,)), ((), ()))
+F32 = jnp.float32
+BF16 = jnp.bfloat16
+MESH_IDS = pl.DeviceIdType.MESH
+
+
+def mm(a, b):
+    return jnp.dot(a, b, preferred_element_type=F32)
+
+
+def layer_kernel(
+    n_tok,
+    n_chip,
+    tokens,
+    routes,
+    route_weights,
+    w_gate,
+    w_up,
+    w_down,
+    enc_hbm,
+    enc_bias,
+    dec_hbm,
+    dec_bias,
+    moe_out,
+    g_enc,
+    g_dec,
+    g_enc_bias,
+    g_dec_bias,
+    loss,
+    wg,
+    wu,
+    wd,
+    enc,
+    dec,
+    tok_all,
+    weight_all,
+    part_send,
+    part_recv,
+    own_pre,
+    hid_send,
+    hid_recv,
+    moe_sib_send,
+    moe_sib_recv,
+    moe_own,
+    moe_z_send,
+    moe_z_recv,
+    moe_all,
+    rec_sib_send,
+    rec_sib_recv,
+    rec_own,
+    rec_dp_send,
+    rec_dp_recv,
+    rec_z_send,
+    rec_z_recv,
+    d_all,
+    tot_send,
+    tot_recv,
+    centered_t,
+    load_sem,
+    send_sem,
+    tok_sem,
+    weight_sem,
+    pair_sem,
+    moe_sem,
+    moe_all_sem,
+    rec_sem,
+    d_all_sem,
+    tot_sem,
+):
+    expert = lax.axis_index("expert")
+    p = lax.axis_index("dp")
+    z, c = expert // 2, expert % 2
+    q, s = 1 - p, 1 - c
+    half = tokens.shape[1]
+    width = 2 * half
+    ff = wg.shape[2]
+    rows = 2 * n_chip * ROWS
+    side = n_chip * ROWS
+
+    loads = []
+    for slot, (hbm, vmem) in enumerate(
+        (
+            (w_gate.at[q], wg.at[0]),
+            (w_up.at[q], wu.at[0]),
+            (w_gate.at[p], wg.at[1]),
+            (w_up.at[p], wu.at[1]),
+            (w_down.at[p], wd.at[1]),
+            (w_down.at[q], wd.at[0]),
+            (dec_hbm, dec),
+            (enc_hbm, enc),
+        )
+    ):
+        load = pltpu.make_async_copy(hbm, vmem, load_sem.at[slot])
+        load.start()
+        loads.append(load)
+
+    sibling = {"expert": z * 2 + s, "dp": p}
+    across = {"expert": expert, "dp": q}
+    chips = [{"expert": lax.rem(z + d, n_chip) * 2 + c, "dp": p} for d in range(n_chip)]
+
+    barrier = pltpu.get_barrier_semaphore()
+    peers = [sibling, across] + chips[1:]
+    for peer in peers:
+        pl.semaphore_signal(barrier, inc=1, device_id=peer, device_id_type=MESH_IDS)
+
+    base = pl.multiple_of((c * n_chip + z) * ROWS, ROWS)
+    block = jnp.concatenate(
+        [tokens[...], jnp.zeros((ROWS - n_tok, half), BF16)], axis=0
+    )
+    tok_all[pl.ds(base, ROWS), :] = block
+    lane = lax.broadcasted_iota(jnp.int32, (n_tok, 128), 1)
+    dense = jnp.zeros((n_tok, 128), F32)
+    for k in range(routes.shape[1]):
+        dense += jnp.where(lane == routes[:, k : k + 1], route_weights[:, k : k + 1], 0.0)
+    weight_all[pl.ds(base, ROWS), :] = jnp.concatenate(
+        [dense, jnp.zeros((ROWS - n_tok, 128), F32)], axis=0
+    )
+    pl.semaphore_wait(barrier, len(peers))
+
+    pending = []
+
+    def send(src, dst, recv, device):
+        copy = pltpu.make_async_remote_copy(
+            src_ref=src,
+            dst_ref=dst,
+            send_sem=send_sem.at[len(pending)],
+            recv_sem=recv,
+            device_id=device,
+            device_id_type=MESH_IDS,
+        )
+        copy.start()
+        pending.append(copy)
+
+    def arrived(dst, recv):
+        pltpu.make_async_remote_copy(
+            src_ref=dst,
+            dst_ref=dst,
+            send_sem=send_sem.at[0],
+            recv_sem=recv,
+            device_id=across,
+            device_id_type=MESH_IDS,
+        ).wait_recv()
+
+    def row_of(zz, cc):
+        return pl.multiple_of((cc * n_chip + zz) * ROWS, ROWS)
+
+    near = [lax.rem(z - d + n_chip, n_chip) for d in range(n_chip)]
+
+    def rows_block(ref, zz, cc):
+        return ref.at[pl.ds(row_of(zz, cc), ROWS), :]
+
+    def gather_rows(pairs):
+        for d in range(1, n_chip):
+            for ref, sem in pairs:
+                blk = rows_block(ref, z, c)
+                send(blk, blk, sem.at[c * n_chip + z], chips[d])
+        for d in range(n_chip):
+            for ref, sem in pairs:
+                blk = rows_block(ref, near[d], c)
+                at = sem.at[c * n_chip + near[d]]
+                if d:
+                    arrived(blk, at)
+                send(blk, blk, at, sibling)
+
+    def finish_rows(ref, sem):
+        for d in range(n_chip):
+            arrived(rows_block(ref, near[d], s), sem.at[s * n_chip + near[d]])
+
+    gather_rows([(tok_all, tok_sem), (weight_all, weight_sem)])
+
+    loads[6].wait()
+    squares = dec[...].astype(F32)
+    norm_col = jnp.sqrt(jnp.sum(squares * squares, axis=1, keepdims=True) + EPSILON)
+    latents = norm_col.shape[0]
+    norm_rows = jnp.broadcast_to(norm_col, (latents, 128)).T
+    norm_row = norm_rows[0:1, :]
+
+    finish_rows(tok_all, tok_sem)
+
+    tile = 256
+    for which, weights in enumerate((wg, wu)):
+        loads[which].wait()
+        for at in range(0, ff, tile):
+            part_send[which, :, at : at + tile] = mm(
+                tok_all[...], weights[0, :, at : at + tile]
+            ).astype(BF16)
+        send(part_send.at[which], part_recv.at[which], pair_sem.at[which], across)
+    for which, weights in enumerate((wg, wu)):
+        loads[2 + which].wait()
+        for at in range(0, ff, tile):
+            own_pre[which, :, at : at + tile] = mm(tok_all[...], weights[1, :, at : at + tile])
+    arrived(part_recv.at[0], pair_sem.at[0])
+    gate = own_pre[0] + part_recv[0].astype(F32)
+    gate = gate / (1.0 + jnp.exp(-gate))
+    arrived(part_recv.at[1], pair_sem.at[1])
+    hid_send[...] = (gate * (own_pre[1] + part_recv[1].astype(F32))).astype(BF16)
+    send(hid_send, hid_recv, pair_sem.at[2], across)
+
+    finish_rows(weight_all, weight_sem)
+    lane_all = lax.broadcasted_iota(jnp.int32, (rows, 128), 1)
+
+    def share_of(index):
+        return jnp.sum(
+            jnp.where(lane_all == expert * 2 + index, weight_all[...], 0.0), axis=1, keepdims=True
+        )
+
+    share_own, share_other = share_of(p), share_of(q)
+    loads[4].wait()
+    moe_own[...] = share_own * mm(hid_send[...], wd[1])
+    loads[5].wait()
+    arrived(hid_recv, pair_sem.at[2])
+    sib_at = pl.multiple_of(s * side, side)
+    own_at = pl.multiple_of(c * side, side)
+    moe_own[...] += share_other * mm(hid_recv[...], wd[0])
+
+    moe_sib_send[...] = moe_own[pl.ds(sib_at, side), :].astype(BF16)
+    send(moe_sib_send, moe_sib_recv, moe_sem.at[n_chip], sibling)
+    arrived(moe_sib_recv, moe_sem.at[n_chip])
+    for d in list(range(1, n_chip)) + [0]:
+        zz = lax.rem(z + d, n_chip)
+        own_rows = pl.ds(pl.multiple_of(zz * ROWS, ROWS), ROWS)
+        total = moe_own[pl.ds(row_of(zz, c), ROWS), :] + moe_sib_recv[own_rows, :].astype(F32)
+        if d:
+            moe_z_send[d] = total.astype(BF16)
+            send(moe_z_send.at[d], moe_z_recv.at[d], moe_sem.at[d], chips[d])
+    for d in range(1, n_chip):
+        arrived(moe_z_recv.at[d], moe_sem.at[d])
+        total += moe_z_recv[d].astype(F32)
+    moe_block = total.astype(BF16)
+    moe_out[...] = moe_block[:n_tok]
+    own_cols = pl.ds(pl.multiple_of(p * half, half), half)
+    other_cols = pl.ds(pl.multiple_of(q * half, half), half)
+    moe_all[pl.ds(base, ROWS), own_cols] = moe_block
+
+    def gather_all(ref, sem):
+        def blk(zz, cc, cols):
+            return ref.at[pl.ds(row_of(zz, cc), ROWS), cols]
+
+        def at(zz, cc, pp):
+            return sem.at[(cc * n_chip + zz) * 2 + pp]
+
+        for d in range(1, n_chip):
+            send(blk(z, c, own_cols), blk(z, c, own_cols), at(z, c, p), chips[d])
+        for zz in near:
+            if zz is not near[0]:
+                arrived(blk(zz, c, own_cols), at(zz, c, p))
+            send(blk(zz, c, own_cols), blk(zz, c, own_cols), at(zz, c, p), across)
+            send(blk(zz, c, own_cols), blk(zz, c, own_cols), at(zz, c, p), sibling)
+        for zz in near:
+            arrived(blk(zz, c, other_cols), at(zz, c, q))
+            send(blk(zz, c, other_cols), blk(zz, c, other_cols), at(zz, c, q), sibling)
+        for zz in near:
+            arrived(blk(zz, s, own_cols), at(zz, s, p))
+            arrived(blk(zz, s, other_cols), at(zz, s, q))
+
+    gather_all(moe_all, moe_all_sem)
+    loads[7].wait()
+    centered = (moe_all[...].astype(F32) - dec_bias[...]).astype(BF16)
+    pre_act = mm(centered, enc[...]) + enc_bias[...]
+    real = lax.broadcasted_iota(jnp.int32, (rows, 1), 0) % ROWS < n_tok
+    scaled = SHARPNESS * pre_act
+    codes = (jnp.maximum(scaled, 0.0) + jnp.log1p(jnp.exp(-jnp.abs(scaled)))) / SHARPNESS
+    codes = jnp.where(real, codes, 0.0)
+    codes_b = codes.astype(BF16)
+
+    rec_own[...] = mm(codes_b, dec[...])
+    rec_sib_send[...] = rec_own[pl.ds(sib_at, side), :].astype(BF16)
+    send(rec_sib_send, rec_sib_recv, rec_sem.at[0], sibling)
+    gates = 1.0 / (1.0 + jnp.exp(-scaled))
+    gates = jnp.where(real, gates, 0.0)
+    arrived(rec_sib_recv, rec_sem.at[0])
+    order = list(range(1, n_chip)) + [0]
+    kept = []
+    for d in order:
+        zz = lax.rem(z + d, n_chip)
+        here = pl.ds(pl.multiple_of(zz * ROWS, ROWS), ROWS)
+        there = pl.ds(row_of(zz, c), ROWS)
+        rec_dp_send[d] = (
+            rec_own[there, other_cols] + rec_sib_recv[here, other_cols].astype(F32)
+        ).astype(BF16)
+        send(rec_dp_send.at[d], rec_dp_recv.at[d], rec_sem.at[1 + d], across)
+        kept.append(rec_own[there, own_cols] + rec_sib_recv[here, own_cols].astype(F32))
+    for d, part in zip(order, kept):
+        arrived(rec_dp_recv.at[d], rec_sem.at[1 + d])
+        recon = part + rec_dp_recv[d].astype(F32)
+        if d:
+            rec_z_send[d] = recon.astype(BF16)
+            send(rec_z_send.at[d], rec_z_recv.at[d], rec_sem.at[1 + n_chip + d], chips[d])
+    centered_t[...] = centered.T
+    codes_t = codes.T
+    code_totals = jnp.sum(codes_t, axis=1, keepdims=True)
+    codes_bt = codes_t.astype(BF16)
+    pull_scale = PENALTY * code_totals / norm_col
+    for d in range(1, n_chip):
+        arrived(rec_z_recv.at[d], rec_sem.at[1 + n_chip + d])
+        recon += rec_z_recv[d].astype(F32)
+    residual = recon + dec_bias[:, own_cols] - moe_all[pl.ds(base, ROWS), own_cols].astype(F32)
+    mine = lax.broadcasted_iota(jnp.int32, (ROWS, 1), 0) < n_tok
+    residual = jnp.where(mine, residual, 0.0)
+    d_all[pl.ds(base, ROWS), own_cols] = (2.0 * residual).astype(BF16)
+    objective = jnp.sum(residual * residual) + PENALTY * jnp.sum(codes * norm_row)
+    gather_all(d_all, d_all_sem)
+
+    d_recon = d_all[...]
+    grad_codes = lax.dot_general(d_recon, dec[...], NT, preferred_element_type=F32)
+    d_pre = (grad_codes + PENALTY * norm_row) * gates
+    d_pre_b = d_pre.astype(BF16)
+    g_enc_bias[...] = jnp.sum(d_pre, axis=0, keepdims=True)
+    totals = jnp.sum(d_pre_b.astype(F32), axis=0, keepdims=True)
+    high = totals.astype(BF16)
+    rest = totals - high.astype(F32)
+    mid = rest.astype(BF16)
+    low = (rest - mid.astype(F32)).astype(BF16)
+    thirds = jnp.concatenate(
+        [high, mid, low, jnp.zeros((ROWS - 3, latents), BF16)], axis=0
+    )
+    pulls = lax.dot_general(thirds, enc[...], NT, preferred_element_type=F32)
+    tot_send[0, :, :width] = jnp.sum(pulls, axis=0, keepdims=True)
+    tot_send[0, :, width:] = jnp.full((1, 128), objective, F32)
+
+    send(tot_send.at[0], tot_recv.at[0], tot_sem.at[0], sibling)
+    mid_at = width // 2
+    g_enc[:mid_at, :] = mm(centered_t[:mid_at, :], d_pre_b).astype(BF16)
+    arrived(tot_recv.at[0], tot_sem.at[0])
+    tot_send[1] = tot_send[0] + tot_recv[0]
+    send(tot_send.at[1], tot_recv.at[1], tot_sem.at[1], across)
+    g_enc[mid_at:, :] = mm(centered_t[mid_at:, :], d_pre_b).astype(BF16)
+    arrived(tot_recv.at[1], tot_sem.at[1])
+    tot_send[2] = tot_send[1] + tot_recv[1]
+    for d in range(1, n_chip):
+        send(tot_send.at[2], tot_recv.at[1 + d], tot_sem.at[1 + d], chips[d])
+    g_dec[...] = (mm(codes_bt, d_recon) + pull_scale * dec[...].astype(F32)).astype(BF16)
+    d_sum = jnp.sum(d_recon.astype(F32), axis=0, keepdims=True)
+    final = tot_send[2]
+    for d in range(1, n_chip):
+        arrived(tot_recv.at[1 + d], tot_sem.at[1 + d])
+        final = final + tot_recv[1 + d]
+    g_dec_bias[...] = d_sum - final[:, :width]
+    loss[...] = final[:, width:] / (n_tok * 2 * n_chip * width)
+    for copy in pending:
+        copy.wait_send()
+
+
+def local_fused(
+    tokens,
+    routes,
+    route_weights,
+    w_gate,
+    w_up,
+    w_down,
+    sae_encoder,
+    enc_bias,
+    sae_decoder,
+    dec_bias,
+):
+    n_tok, half = tokens.shape
+    n_chip = lax.axis_size("expert") // 2
+    width = 2 * half
+    ff = w_gate.shape[2]
+    latents = enc_bias.shape[0]
+    side = n_chip * ROWS
+    rows = 2 * side
+    vmem = pl.BlockSpec(memory_space=pltpu.VMEM)
+    hbm = pl.BlockSpec(memory_space=pl.ANY)
+    dma = pltpu.SemaphoreType.DMA
+    scratch = [
+        pltpu.VMEM((2, half, ff), BF16),
+        pltpu.VMEM((2, half, ff), BF16),
+        pltpu.VMEM((2, ff, half), BF16),
+        pltpu.VMEM((width, latents), BF16),
+        pltpu.VMEM((latents, width), BF16),
+        pltpu.VMEM((rows, half), BF16),
+        pltpu.VMEM((rows, 128), F32),
+        pltpu.VMEM((2, rows, ff), BF16),
+        pltpu.VMEM((2, rows, ff), BF16),
+        pltpu.VMEM((2, rows, ff), F32),
+        pltpu.VMEM((rows, ff), BF16),
+        pltpu.VMEM((rows, ff), BF16),
+        pltpu.VMEM((side, half), BF16),
+        pltpu.VMEM((side, half), BF16),
+        pltpu.VMEM((rows, half), F32),
+        pltpu.VMEM((n_chip, ROWS, half), BF16),
+        pltpu.VMEM((n_chip, ROWS, half), BF16),
+        pltpu.VMEM((rows, width), BF16),
+        pltpu.VMEM((side, width), BF16),
+        pltpu.VMEM((side, width), BF16),
+        pltpu.VMEM((rows, width), F32),
+        pltpu.VMEM((n_chip, ROWS, half), BF16),
+        pltpu.VMEM((n_chip, ROWS, half), BF16),
+        pltpu.VMEM((n_chip, ROWS, half), BF16),
+        pltpu.VMEM((n_chip, ROWS, half), BF16),
+        pltpu.VMEM((rows, width), BF16),
+        pltpu.VMEM((3, 1, width + 128), F32),
+        pltpu.VMEM((1 + n_chip, 1, width + 128), F32),
+        pltpu.VMEM((width, rows), BF16),
+        dma((8,)),
+        dma((16 * n_chip,)),
+        dma((2 * n_chip,)),
+        dma((2 * n_chip,)),
+        dma((3,)),
+        dma((n_chip + 1,)),
+        dma((4 * n_chip,)),
+        dma((1 + 2 * n_chip,)),
+        dma((4 * n_chip,)),
+        dma((1 + n_chip,)),
+    ]
+    outs = pl.pallas_call(
+        functools.partial(layer_kernel, n_tok, n_chip),
+        out_shape=(
+            jax.ShapeDtypeStruct((n_tok, half), BF16),
+            jax.ShapeDtypeStruct((width, latents), BF16),
+            jax.ShapeDtypeStruct((latents, width), BF16),
+            jax.ShapeDtypeStruct((1, latents), F32),
+            jax.ShapeDtypeStruct((1, width), F32),
+            jax.ShapeDtypeStruct((1, 128), F32),
+        ),
+        in_specs=[vmem, vmem, vmem, hbm, hbm, hbm, hbm, vmem, hbm, vmem],
+        out_specs=(vmem,) * 6,
+        scratch_shapes=scratch,
+        compiler_params=pltpu.CompilerParams(
+            collective_id=0, has_side_effects=True, vmem_limit_bytes=48 * 1024 * 1024
+        ),
+    )(
+        tokens,
+        routes,
+        route_weights,
+        w_gate,
+        w_up,
+        w_down,
+        sae_encoder,
+        enc_bias.reshape(1, -1),
+        sae_decoder,
+        dec_bias.reshape(1, -1),
+    )
+    moe_out, g_enc, g_dec, g_enc_bias, g_dec_bias, loss = outs
+    return moe_out, g_enc, g_dec, g_enc_bias.reshape(-1), g_dec_bias.reshape(-1), loss[0, :1]
+
+
+def local(*args):
+    tokens, w_gate = args[0], args[3]
+    pairs = lax.axis_size("dp") == 2 and w_gate.shape[0] == 2
+    total_experts = 2 * lax.axis_size("expert")
+    if pairs and lax.axis_size("expert") % 2 == 0 and total_experts <= 32 and tokens.shape[0] <= ROWS:
+        return local_fused(*args)
+    return local_plain(*args)
+
+
 def solution(mesh):
     in_specs = (
         P(("groups", "expert"), "dp"),

time: 245 us -> 82.2 us (0.34)
  blocking collectives: 113 us -> 0 us
  Pallas kernels: 0 us -> 69.9 us
  waiting for transfers between devices: 67.6 us -> 0 us
  matrix products: 20.9 us -> 0 us
  between operations: 18 us -> 1.83 us
  starting transfers between devices: 5.97 us -> 0 us
  other arithmetic: 5.82 us -> 0 us
    pallas_call x0 -> x1, Pallas kernels: none -> 69.9 us  [local_fused(): pl.pallas_call(functools.partial(layer_kernel, n_tok, n_chip), out_shape=...]
    psum x1 -> x0, waiting for transfers between devices: 50.7 us -> none  [local(): gate_full, up_full = lax.psum((gate_part, up_part), 'dp')]
    all_gather x4 -> x0, blocking collectives: 40.9 us -> none  [the longest x2 31.6 us: gather_tokens(): return lax.all_gather(widened, 'expert', axis=0, tiled=True)]
    psum x1 -> x0, blocking collectives: 34.4 us -> none  [local(): lax.psum((bias_pull, objective_part), ('expert', 'dp'))]
    dot_general x11 -> x0, matrix products: 20.9 us -> none  [the longest x1 3.4 us: local(): jnp.einsum('secd,edf->secf', received, w_gate, preferred_element_type=jnp...]
    unnamed x1 -> x0, blocking collectives: 19.6 us -> none
    all_to_all x1 -> x0, blocking collectives: 18 us -> none  [local(): lax.all_to_all(send_blocks, 'expert', split_axis=0, concat_axis=0, tiled=...]
    all_to_all x1 -> x0, waiting for transfers between devices: 9.63 us -> none  [local(): lax.all_to_all(outputs.astype(jnp.bfloat16), 'expert', split_axis=0, conc...]
  transfers between devices with their start and end apart: 4 -> 0, of which waited for: 3 -> 0; matrix products, arithmetic and copies ran while one was open for 1% -> 0% of each run, Pallas kernels for 0% -> 0%
where the time goes in v1:
time: 82.2 us; the launch traced here: 81.8 us
  Pallas kernels  69.9 us (85%)
  local copies, waits for them, and re-layouts  10.1 us (12%)
  between operations  1.83 us (2%)
    pallas_call x1, Pallas kernels, local_fused(): pl.pallas_call(functools.partial(layer_kernel, n_tok, n_chip), out_shape=...  69.9 us
    unnamed x16, local copies, waits for them, and re-layouts  10.1 us

profile of v1, /device:TPU:0, one launch (start us, length us, event | category | flops | bytes accessed | tf_op | source)
XLA Modules:
  0.0 81.8 jit_solution(11788560805636012537)
XLA Ops:
  0.6 0.8 copy.16.routes
  1.4 0.8 copy.17.route_weights
  2.2 1.4 %copy.18.enc_hbm = bf16[2048,192]{1,0:T(8,128)(2,1)S(1)} copy(bf16[2048,192]{0,1:T(8,128)(2,1)} %param.16) | data formatting | bytes 1572864 | tf_op args[6]
  3.6 0.0 copy-start
  3.6 1.1 %copy-done = bf16[192,2048]{1,0:T(8,128)(2,1)S(1)} copy-done((bf16[192,2048]{1,0:T(8,128)(2,1)S(1)}, bf16[192,2048]{1,0:T(8,128)(2,1)}, u32[]{:S(2)}) %copy-start) | copy-done | bytes 786456
  4.7 0.0 copy-start.1
  4.7 0.8 copy-done.1
  5.5 0.0 copy-start.2
  5.5 0.7 copy-done.2
  6.2 0.0 copy-start.3
  6.2 0.7 copy-done.3
  6.9 69.9 %shard_map.145 = (bf16[15,1024]{1,0:T(8,128)(2,1)S(1)}, bf16[2048,192]{1,0:T(8,128)(2,1)S(1)}, bf16[192,2048]{1,0:T(8,128)(2,1)S(1)}, f32[1,192]{1,0:T(1,128)S(1...) custom-call(bf16[15,1024]{1,0:T(8,128)(2,1)S(1)} %copy-done.1, s32[15,8]{1,0:T(8,128)S(1)} %copy.16.routes, ...), custom_call_target="tpu_custom_call" | custom-call | tf_op jit(solution)/shard_map/pallas_call | solution.py:529
  76.8 1.2 %copy.19 = bf16[2048,192]{0,1:T(8,128)(2,1)} copy(bf16[2048,192]{1,0:T(8,128)(2,1)S(1)} %get-tuple-element.19) | data formatting | bytes 1572864
  78.0 0.6 copy.25
  78.6 0.9 %copy.26 = bf16[192,2048]{1,0:T(8,128)(2,1)} copy(bf16[192,2048]{1,0:T(8,128)(2,1)S(1)} %get-tuple-element.32) | data formatting | bytes 1572864
  79.5 0.6 copy.27
  80.1 0.6 copy.28
Async XLA Ops:
  3.6 1.1 %copy-start = (bf16[192,2048]{1,0:T(8,128)(2,1)S(1)}, bf16[192,2048]{1,0:T(8,128)(2,1)}, u32[]{:S(2)}) copy-start(bf16[192,2048]{1,0:T(8,128)(2,1)} %dec_hbm.1) | copy-start | bytes 2359300
  4.7 0.8 copy-start.1
  5.5 0.7 copy-start.2
  6.2 0.7 copy-start.3

commit v2 on v1

--- a/solution.py
+++ b/solution.py
@@ -133,22 +133,33 @@
 def layer_kernel(
     n_tok,
     n_chip,
-    tokens,
-    routes,
-    route_weights,
+    tok_hbm,
+    routes_hbm,
+    route_weights_hbm,
     w_gate,
     w_up,
     w_down,
     enc_hbm,
-    enc_bias,
+    enc_bias_hbm,
     dec_hbm,
-    dec_bias,
+    dec_bias_hbm,
+    moe_hbm,
+    g_enc_hbm,
+    g_dec_hbm,
+    g_enc_bias_hbm,
+    g_dec_bias_hbm,
+    loss_hbm,
     moe_out,
     g_enc,
     g_dec,
     g_enc_bias,
     g_dec_bias,
     loss,
+    tokens,
+    routes,
+    route_weights,
+    enc_bias,
+    dec_bias,
     wg,
     wu,
     wd,
@@ -177,7 +188,7 @@
     d_all,
     tot_send,
     tot_recv,
-    centered_t,
+    centered_ref,
     load_sem,
     send_sem,
     tok_sem,
@@ -188,6 +199,7 @@
     rec_sem,
     d_all_sem,
     tot_sem,
+    store_sem,
 ):
     expert = lax.axis_index("expert")
     p = lax.axis_index("dp")
@@ -196,12 +208,17 @@
     half = tokens.shape[1]
     width = 2 * half
     ff = wg.shape[2]
+    tile = part_send.shape[-1]
+    tiles = ff // tile
     rows = 2 * n_chip * ROWS
     side = n_chip * ROWS
 
     loads = []
     for slot, (hbm, vmem) in enumerate(
         (
+            (tok_hbm, tokens),
+            (routes_hbm, routes),
+            (route_weights_hbm, route_weights),
             (w_gate.at[q], wg.at[0]),
             (w_up.at[q], wu.at[0]),
             (w_gate.at[p], wg.at[1]),
@@ -210,6 +227,8 @@
             (w_down.at[q], wd.at[0]),
             (dec_hbm, dec),
             (enc_hbm, enc),
+            (enc_bias_hbm, enc_bias),
+            (dec_bias_hbm, dec_bias),
         )
     ):
         load = pltpu.make_async_copy(hbm, vmem, load_sem.at[slot])
@@ -221,25 +240,37 @@
     chips = [{"expert": lax.rem(z + d, n_chip) * 2 + c, "dp": p} for d in range(n_chip)]
 
     barrier = pltpu.get_barrier_semaphore()
-    peers = [sibling, across] + chips[1:]
+    diagonal = {"expert": z * 2 + s, "dp": q}
+    peers = [sibling, across, diagonal] + chips[1:]
     for peer in peers:
         pl.semaphore_signal(barrier, inc=1, device_id=peer, device_id_type=MESH_IDS)
 
     base = pl.multiple_of((c * n_chip + z) * ROWS, ROWS)
+    loads[0].wait()
     block = jnp.concatenate(
         [tokens[...], jnp.zeros((ROWS - n_tok, half), BF16)], axis=0
     )
     tok_all[pl.ds(base, ROWS), :] = block
-    lane = lax.broadcasted_iota(jnp.int32, (n_tok, 128), 1)
-    dense = jnp.zeros((n_tok, 128), F32)
-    for k in range(routes.shape[1]):
-        dense += jnp.where(lane == routes[:, k : k + 1], route_weights[:, k : k + 1], 0.0)
-    weight_all[pl.ds(base, ROWS), :] = jnp.concatenate(
-        [dense, jnp.zeros((ROWS - n_tok, 128), F32)], axis=0
-    )
+    loads[1].wait()
+    loads[2].wait()
+    wide = (128, 128)
+    fill = jnp.zeros((routes.shape[0], 128 - n_tok), jnp.int32)
+    named = jnp.concatenate([routes[...], fill], axis=1)
+    given = jnp.concatenate([route_weights[...], fill.astype(F32)], axis=1)
+    of_expert = lax.broadcasted_iota(jnp.int32, wide, 0)
+    dense = jnp.zeros(wide, F32)
+    for k in range(routes.shape[0]):
+        dense += jnp.where(of_expert == named[k : k + 1, :], given[k : k + 1, :], 0.0)
+    weight_all[pl.ds(base, ROWS), :] = dense.T[:ROWS, :]
     pl.semaphore_wait(barrier, len(peers))
 
     pending = []
+    stores = []
+
+    def store(vmem, hbm):
+        copy = pltpu.make_async_copy(vmem, hbm, store_sem.at[len(stores)])
+        copy.start()
+        stores.append(copy)
 
     def send(src, dst, recv, device):
         copy = pltpu.make_async_remote_copy(
@@ -290,7 +321,7 @@
 
     gather_rows([(tok_all, tok_sem), (weight_all, weight_sem)])
 
-    loads[6].wait()
+    loads[9].wait()
     squares = dec[...].astype(F32)
     norm_col = jnp.sqrt(jnp.sum(squares * squares, axis=1, keepdims=True) + EPSILON)
     latents = norm_col.shape[0]
@@ -299,24 +330,19 @@
 
     finish_rows(tok_all, tok_sem)
 
-    tile = 256
-    for which, weights in enumerate((wg, wu)):
-        loads[which].wait()
-        for at in range(0, ff, tile):
-            part_send[which, :, at : at + tile] = mm(
-                tok_all[...], weights[0, :, at : at + tile]
-            ).astype(BF16)
-        send(part_send.at[which], part_recv.at[which], pair_sem.at[which], across)
-    for which, weights in enumerate((wg, wu)):
-        loads[2 + which].wait()
-        for at in range(0, ff, tile):
-            own_pre[which, :, at : at + tile] = mm(tok_all[...], weights[1, :, at : at + tile])
-    arrived(part_recv.at[0], pair_sem.at[0])
-    gate = own_pre[0] + part_recv[0].astype(F32)
-    gate = gate / (1.0 + jnp.exp(-gate))
-    arrived(part_recv.at[1], pair_sem.at[1])
-    hid_send[...] = (gate * (own_pre[1] + part_recv[1].astype(F32))).astype(BF16)
-    send(hid_send, hid_recv, pair_sem.at[2], across)
+    loads[3].wait()
+    loads[4].wait()
+    for t in range(tiles):
+        cols = slice(t * tile, (t + 1) * tile)
+        for which, weights in enumerate((wg, wu)):
+            part_send[t, which] = mm(tok_all[...], weights[0, :, cols]).astype(BF16)
+        send(part_send.at[t], part_recv.at[t], pair_sem.at[t], across)
+    loads[5].wait()
+    loads[6].wait()
+    for t in range(tiles):
+        cols = slice(t * tile, (t + 1) * tile)
+        for which, weights in enumerate((wg, wu)):
+            own_pre[t, which] = mm(tok_all[...], weights[1, :, cols])
 
     finish_rows(weight_all, weight_sem)
     lane_all = lax.broadcasted_iota(jnp.int32, (rows, 128), 1)
@@ -327,13 +353,23 @@
         )
 
     share_own, share_other = share_of(p), share_of(q)
-    loads[4].wait()
-    moe_own[...] = share_own * mm(hid_send[...], wd[1])
-    loads[5].wait()
-    arrived(hid_recv, pair_sem.at[2])
+    for t in range(tiles):
+        arrived(part_recv.at[t], pair_sem.at[t])
+        gate = own_pre[t, 0] + part_recv[t, 0].astype(F32)
+        up = own_pre[t, 1] + part_recv[t, 1].astype(F32)
+        hid_send[t] = (gate / (1.0 + jnp.exp(-gate)) * up).astype(BF16)
+        send(hid_send.at[t], hid_recv.at[t], pair_sem.at[tiles + t], across)
+
     sib_at = pl.multiple_of(s * side, side)
-    own_at = pl.multiple_of(c * side, side)
-    moe_own[...] += share_other * mm(hid_recv[...], wd[0])
+    loads[7].wait()
+    loads[8].wait()
+    down = mm(hid_send[0], wd[1, :tile])
+    for t in range(1, tiles):
+        down += mm(hid_send[t], wd[1, t * tile : (t + 1) * tile])
+    moe_own[...] = share_own * down
+    for t in range(tiles):
+        arrived(hid_recv.at[t], pair_sem.at[tiles + t])
+        moe_own[...] += share_other * mm(hid_recv[t], wd[0, t * tile : (t + 1) * tile])
 
     moe_sib_send[...] = moe_own[pl.ds(sib_at, side), :].astype(BF16)
     send(moe_sib_send, moe_sib_recv, moe_sem.at[n_chip], sibling)
@@ -350,6 +386,7 @@
         total += moe_z_recv[d].astype(F32)
     moe_block = total.astype(BF16)
     moe_out[...] = moe_block[:n_tok]
+    store(moe_out, moe_hbm)
     own_cols = pl.ds(pl.multiple_of(p * half, half), half)
     other_cols = pl.ds(pl.multiple_of(q * half, half), half)
     moe_all[pl.ds(base, ROWS), own_cols] = moe_block
@@ -376,9 +413,10 @@
             arrived(blk(zz, s, other_cols), at(zz, s, q))
 
     gather_all(moe_all, moe_all_sem)
-    loads[7].wait()
+    for slot in (10, 11, 12):
+        loads[slot].wait()
     centered = (moe_all[...].astype(F32) - dec_bias[...]).astype(BF16)
-    pre_act = mm(centered, enc[...]) + enc_bias[...]
+    pre_act = lax.dot_general(centered, enc[...], NT, preferred_element_type=F32) + enc_bias[...]
     real = lax.broadcasted_iota(jnp.int32, (rows, 1), 0) % ROWS < n_tok
     scaled = SHARPNESS * pre_act
     codes = (jnp.maximum(scaled, 0.0) + jnp.log1p(jnp.exp(-jnp.abs(scaled)))) / SHARPNESS
@@ -408,7 +446,7 @@
         if d:
             rec_z_send[d] = recon.astype(BF16)
             send(rec_z_send.at[d], rec_z_recv.at[d], rec_sem.at[1 + n_chip + d], chips[d])
-    centered_t[...] = centered.T
+    centered_ref[...] = centered
     codes_t = codes.T
     code_totals = jnp.sum(codes_t, axis=1, keepdims=True)
     codes_bt = codes_t.astype(BF16)
@@ -428,6 +466,7 @@
     d_pre = (grad_codes + PENALTY * norm_row) * gates
     d_pre_b = d_pre.astype(BF16)
     g_enc_bias[...] = jnp.sum(d_pre, axis=0, keepdims=True)
+    store(g_enc_bias, g_enc_bias_hbm)
     totals = jnp.sum(d_pre_b.astype(F32), axis=0, keepdims=True)
     high = totals.astype(BF16)
     rest = totals - high.astype(F32)
@@ -436,31 +475,53 @@
     thirds = jnp.concatenate(
         [high, mid, low, jnp.zeros((ROWS - 3, latents), BF16)], axis=0
     )
-    pulls = lax.dot_general(thirds, enc[...], NT, preferred_element_type=F32)
+    pulls = mm(thirds, enc[...])
     tot_send[0, :, :width] = jnp.sum(pulls, axis=0, keepdims=True)
     tot_send[0, :, width:] = jnp.full((1, 128), objective, F32)
 
-    send(tot_send.at[0], tot_recv.at[0], tot_sem.at[0], sibling)
-    mid_at = width // 2
-    g_enc[:mid_at, :] = mm(centered_t[:mid_at, :], d_pre_b).astype(BF16)
-    arrived(tot_recv.at[0], tot_sem.at[0])
-    tot_send[1] = tot_send[0] + tot_recv[0]
-    send(tot_send.at[1], tot_recv.at[1], tot_sem.at[1], across)
-    g_enc[mid_at:, :] = mm(centered_t[mid_at:, :], d_pre_b).astype(BF16)
-    arrived(tot_recv.at[1], tot_sem.at[1])
-    tot_send[2] = tot_send[1] + tot_recv[1]
+    for slot, device in enumerate((sibling, across, diagonal)):
+        send(tot_send.at[0], tot_recv.at[slot], tot_sem.at[slot], device)
+    d_pre_t = d_pre.T.astype(BF16)
+    g_enc[...] = mm(d_pre_t, centered_ref[...]).astype(BF16)
+    store(g_enc, g_enc_hbm)
+    total = tot_send[0]
+    for slot in range(3):
+        arrived(tot_recv.at[slot], tot_sem.at[slot])
+        total = total + tot_recv[slot]
+    tot_send[1] = total
     for d in range(1, n_chip):
-        send(tot_send.at[2], tot_recv.at[1 + d], tot_sem.at[1 + d], chips[d])
+        send(tot_send.at[1], tot_recv.at[2 + d], tot_sem.at[2 + d], chips[d])
     g_dec[...] = (mm(codes_bt, d_recon) + pull_scale * dec[...].astype(F32)).astype(BF16)
+    store(g_dec, g_dec_hbm)
     d_sum = jnp.sum(d_recon.astype(F32), axis=0, keepdims=True)
-    final = tot_send[2]
+    final = total
     for d in range(1, n_chip):
-        arrived(tot_recv.at[1 + d], tot_sem.at[1 + d])
-        final = final + tot_recv[1 + d]
+        arrived(tot_recv.at[2 + d], tot_sem.at[2 + d])
+        final = final + tot_recv[2 + d]
     g_dec_bias[...] = d_sum - final[:, :width]
     loss[...] = final[:, width:] / (n_tok * 2 * n_chip * width)
+    store(g_dec_bias, g_dec_bias_hbm)
+    store(loss, loss_hbm)
     for copy in pending:
         copy.wait_send()
+    for copy in stores:
+        copy.wait()
+
+
+def hand_over(count, *refs):
+    held = refs[2 * count : 3 * count]
+    sems = refs[-1]
+    reads = [pltpu.make_async_copy(refs[i], held[i], sems.at[i]) for i in range(count)]
+    writes = [
+        pltpu.make_async_copy(held[i], refs[count + i], sems.at[count + i]) for i in range(count)
+    ]
+    for copy in reads:
+        copy.start()
+    for read, write in zip(reads, writes):
+        read.wait()
+        write.start()
+    for copy in writes:
+        copy.wait()
 
 
 def local_fused(
@@ -482,22 +543,37 @@
     latents = enc_bias.shape[0]
     side = n_chip * ROWS
     rows = 2 * side
-    vmem = pl.BlockSpec(memory_space=pltpu.VMEM)
-    hbm = pl.BlockSpec(memory_space=pl.ANY)
+    tile = 256 if ff % 256 == 0 else ff
+    tiles = ff // tile
+    top = routes.shape[1]
+    hbm = pl.BlockSpec(memory_space=pltpu.HBM)
     dma = pltpu.SemaphoreType.DMA
-    scratch = [
+    shapes = (
+        jax.ShapeDtypeStruct((n_tok, half), BF16),
+        jax.ShapeDtypeStruct((latents, width), BF16),
+        jax.ShapeDtypeStruct((latents, width), BF16),
+        jax.ShapeDtypeStruct((1, latents), F32),
+        jax.ShapeDtypeStruct((1, width), F32),
+        jax.ShapeDtypeStruct((1, 128), F32),
+    )
+    scratch = [pltpu.VMEM(out.shape, out.dtype) for out in shapes] + [
+        pltpu.VMEM((n_tok, half), BF16),
+        pltpu.VMEM((top, n_tok), jnp.int32),
+        pltpu.VMEM((top, n_tok), F32),
+        pltpu.VMEM((1, latents), F32),
+        pltpu.VMEM((1, width), F32),
         pltpu.VMEM((2, half, ff), BF16),
         pltpu.VMEM((2, half, ff), BF16),
         pltpu.VMEM((2, ff, half), BF16),
-        pltpu.VMEM((width, latents), BF16),
+        pltpu.VMEM((latents, width), BF16),
         pltpu.VMEM((latents, width), BF16),
         pltpu.VMEM((rows, half), BF16),
         pltpu.VMEM((rows, 128), F32),
-        pltpu.VMEM((2, rows, ff), BF16),
-        pltpu.VMEM((2, rows, ff), BF16),
-        pltpu.VMEM((2, rows, ff), F32),
-        pltpu.VMEM((rows, ff), BF16),
-        pltpu.VMEM((rows, ff), BF16),
+        pltpu.VMEM((tiles, 2, rows, tile), BF16),
+        pltpu.VMEM((tiles, 2, rows, tile), BF16),
+        pltpu.VMEM((tiles, 2, rows, tile), F32),
+        pltpu.VMEM((tiles, rows, tile), BF16),
+        pltpu.VMEM((tiles, rows, tile), BF16),
         pltpu.VMEM((side, half), BF16),
         pltpu.VMEM((side, half), BF16),
         pltpu.VMEM((rows, half), F32),
@@ -512,50 +588,52 @@
         pltpu.VMEM((n_chip, ROWS, half), BF16),
         pltpu.VMEM((n_chip, ROWS, half), BF16),
         pltpu.VMEM((rows, width), BF16),
-        pltpu.VMEM((3, 1, width + 128), F32),
-        pltpu.VMEM((1 + n_chip, 1, width + 128), F32),
-        pltpu.VMEM((width, rows), BF16),
-        dma((8,)),
-        dma((16 * n_chip,)),
+        pltpu.VMEM((2, 1, width + 128), F32),
+        pltpu.VMEM((2 + n_chip, 1, width + 128), F32),
+        pltpu.VMEM((rows, width), BF16),
+        dma((13,)),
+        dma((16 * n_chip + 2 * tiles,)),
         dma((2 * n_chip,)),
         dma((2 * n_chip,)),
-        dma((3,)),
+        dma((2 * tiles,)),
         dma((n_chip + 1,)),
         dma((4 * n_chip,)),
         dma((1 + 2 * n_chip,)),
         dma((4 * n_chip,)),
-        dma((1 + n_chip,)),
+        dma((2 + n_chip,)),
+        dma((len(shapes),)),
     ]
     outs = pl.pallas_call(
         functools.partial(layer_kernel, n_tok, n_chip),
-        out_shape=(
-            jax.ShapeDtypeStruct((n_tok, half), BF16),
-            jax.ShapeDtypeStruct((width, latents), BF16),
-            jax.ShapeDtypeStruct((latents, width), BF16),
-            jax.ShapeDtypeStruct((1, latents), F32),
-            jax.ShapeDtypeStruct((1, width), F32),
-            jax.ShapeDtypeStruct((1, 128), F32),
-        ),
-        in_specs=[vmem, vmem, vmem, hbm, hbm, hbm, hbm, vmem, hbm, vmem],
-        out_specs=(vmem,) * 6,
+        out_shape=shapes,
+        in_specs=[hbm] * 10,
+        out_specs=(hbm,) * 6,
         scratch_shapes=scratch,
         compiler_params=pltpu.CompilerParams(
-            collective_id=0, has_side_effects=True, vmem_limit_bytes=48 * 1024 * 1024
+            collective_id=0, has_side_effects=True, vmem_limit_bytes=63 * 1024 * 1024
         ),
     )(
         tokens,
-        routes,
-        route_weights,
+        routes.T,
+        route_weights.T,
         w_gate,
         w_up,
         w_down,
-        sae_encoder,
+        sae_encoder.T,
         enc_bias.reshape(1, -1),
         sae_decoder,
         dec_bias.reshape(1, -1),
     )
-    moe_out, g_enc, g_dec, g_enc_bias, g_dec_bias, loss = outs
-    return moe_out, g_enc, g_dec, g_enc_bias.reshape(-1), g_dec_bias.reshape(-1), loss[0, :1]
+    moe_out, g_enc, g_dec, g_enc_bias, g_dec_bias, loss = pl.pallas_call(
+        functools.partial(hand_over, len(shapes)),
+        out_shape=shapes,
+        in_specs=[hbm] * len(shapes),
+        out_specs=(hbm,) * len(shapes),
+        scratch_shapes=[pltpu.VMEM(out.shape, out.dtype) for out in shapes]
+        + [dma((2 * len(shapes),))],
+        compiler_params=pltpu.CompilerParams(vmem_limit_bytes=63 * 1024 * 1024),
+    )(*outs)
+    return moe_out, g_enc.T, g_dec, g_enc_bias.reshape(-1), g_dec_bias.reshape(-1), loss[0, :1]
 
 
 def local(*args):

time: 82.2 us -> 70.6 us (0.86)
  local copies, waits for them, and re-layouts: 10.1 us -> 0 us
  between operations: 1.83 us -> 0.64 us
    unnamed x16 -> x0, local copies, waits for them, and re-layouts: 10.1 us -> none
    pallas_call x1, Pallas kernels: 69.9 us -> 67.4 us  [local_fused(): pl.pallas_call(functools.partial(layer_kernel, n_tok, n_chip), out_shape=...]
    pallas_call x0 -> x1, Pallas kernels: none -> 2.4 us  [local_fused(): pl.pallas_call(functools.partial(hand_over, len(shapes)), out_shape=shape...]
where the time goes in v2:
time: 70.6 us; the launch traced here: 70.4 us
  Pallas kernels  69.8 us (99%)
    pallas_call x1, Pallas kernels, local_fused(): pl.pallas_call(functools.partial(layer_kernel, n_tok, n_chip), out_shape=...  67.4 us
    pallas_call x1, Pallas kernels, local_fused(): pl.pallas_call(functools.partial(hand_over, len(shapes)), out_shape=shape...  2.4 us

profile of v2, /device:TPU:0, one launch (start us, length us, event | category | flops | bytes accessed | tf_op | source)
XLA Modules:
  0.0 70.4 jit_solution(8257610721399186409)
XLA Ops:
  0.6 67.4 %shard_map.145 = (bf16[15,1024]{1,0:T(8,128)(2,1)}, bf16[192,2048]{1,0:T(8,128)(2,1)}, bf16[192,2048]{1,0:T(8,128)(2,1)}, f32[1,192]{1,0:T(1,128)}, f32[1,2048]{1,0:T(1,128)}, /*index=5*/f32[1,128]{1,0:T(1,128)}) custom-call(bf16[15,1024]{1,0:T(8,128)(2,1)} %tok_hbm.1, s32[8,15]{1,0:T(8,128)} %bitcast.12, f32[8,15]{1,0:T(8,128)} %bitcast.13, ...), custom_call_target="tpu_custom_call" | custom-call | tf_op jit(solution)/shard_map/pallas_call | solution.py:606
  68.0 2.4 %shard_map.146 = (bf16[15,1024]{1,0:T(8,128)(2,1)}, bf16[192,2048]{1,0:T(8,128)(2,1)}, bf16[192,2048]{1,0:T(8,128)(2,1)}, f32[1,192]{1,0:T(1,128)}, f32[1,2048]{1,0:T(1,128)}, /*index=5*/f32[1,128]{1,0:T(1,128)}) custom-call(bf16[15,1024]{1,0:T(8,128)(2,1)} %get-tuple-element.18.refs_0_, bf16[192,2048]{1,0:T(8,128)(2,1)} %get-tuple-element.19.refs_1_, ...), custom_call_target="tpu_custom_call" | custom-call | tf_op jit(solution)/shard_map/pallas_call | solution.py:627

commit v3 on v2

--- a/solution.py
+++ b/solution.py
@@ -167,6 +167,7 @@
     dec,
     tok_all,
     weight_all,
+    picked,
     part_send,
     part_recv,
     own_pre,
@@ -328,31 +329,45 @@
     norm_rows = jnp.broadcast_to(norm_col, (latents, 128)).T
     norm_row = norm_rows[0:1, :]
 
+    finish_rows(weight_all, weight_sem)
+    slots = picked.shape[1]
+    by_expert = weight_all[...].T
+    of_row = lax.broadcasted_iota(jnp.int32, by_expert.shape, 0)
+    lane_all = lax.broadcasted_iota(jnp.int32, (rows, 128), 1)
+    before = lax.broadcasted_iota(jnp.int32, (rows, rows), 0)
+    before = (before < lax.broadcasted_iota(jnp.int32, (rows, rows), 1)).astype(BF16)
+    slot_of = lax.broadcasted_iota(jnp.int32, (slots, rows), 0).astype(F32)
+    shares, hots = [], []
+    for index in (q, p):
+        number = expert * 2 + index
+        given_row = jnp.sum(jnp.where(of_row == number, by_expert, 0.0), axis=0, keepdims=True)
+        named_row = jnp.where(given_row > 0.0, 1.0, 0.0)
+        place = mm(jnp.broadcast_to(named_row, (ROWS, rows)).astype(BF16), before)[0:1, :]
+        place = jnp.where(given_row > 0.0, place, -1.0)
+        hots.append(jnp.where(slot_of == place, 1.0, 0.0))
+        shares.append(
+            jnp.sum(jnp.where(lane_all == number, weight_all[...], 0.0), axis=1, keepdims=True)
+        )
+    share_other, share_own = shares
+    back_other, back_own = [hot.T.astype(BF16) for hot in hots]
     finish_rows(tok_all, tok_sem)
+    picked[0] = mm(hots[0].astype(BF16), tok_all[...]).astype(BF16)
 
     loads[3].wait()
     loads[4].wait()
     for t in range(tiles):
         cols = slice(t * tile, (t + 1) * tile)
         for which, weights in enumerate((wg, wu)):
-            part_send[t, which] = mm(tok_all[...], weights[0, :, cols]).astype(BF16)
+            part_send[t, which] = mm(picked[0], weights[0, :, cols]).astype(BF16)
         send(part_send.at[t], part_recv.at[t], pair_sem.at[t], across)
+    picked[1] = mm(hots[1].astype(BF16), tok_all[...]).astype(BF16)
     loads[5].wait()
     loads[6].wait()
     for t in range(tiles):
         cols = slice(t * tile, (t + 1) * tile)
         for which, weights in enumerate((wg, wu)):
-            own_pre[t, which] = mm(tok_all[...], weights[1, :, cols])
-
-    finish_rows(weight_all, weight_sem)
-    lane_all = lax.broadcasted_iota(jnp.int32, (rows, 128), 1)
-
-    def share_of(index):
-        return jnp.sum(
-            jnp.where(lane_all == expert * 2 + index, weight_all[...], 0.0), axis=1, keepdims=True
-        )
-
-    share_own, share_other = share_of(p), share_of(q)
+            own_pre[t, which] = mm(picked[1], weights[1, :, cols])
+
     for t in range(tiles):
         arrived(part_recv.at[t], pair_sem.at[t])
         gate = own_pre[t, 0] + part_recv[t, 0].astype(F32)
@@ -366,10 +381,13 @@
     down = mm(hid_send[0], wd[1, :tile])
     for t in range(1, tiles):
         down += mm(hid_send[t], wd[1, t * tile : (t + 1) * tile])
-    moe_own[...] = share_own * down
-    for t in range(tiles):
+    moe_own[...] = share_own * mm(back_own, down.astype(BF16))
+    arrived(hid_recv.at[0], pair_sem.at[tiles])
+    down = mm(hid_recv[0], wd[0, :tile])
+    for t in range(1, tiles):
         arrived(hid_recv.at[t], pair_sem.at[tiles + t])
-        moe_own[...] += share_other * mm(hid_recv[t], wd[0, t * tile : (t + 1) * tile])
+        down += mm(hid_recv[t], wd[0, t * tile : (t + 1) * tile])
+    moe_own[...] += share_other * mm(back_other, down.astype(BF16))
 
     moe_sib_send[...] = moe_own[pl.ds(sib_at, side), :].astype(BF16)
     send(moe_sib_send, moe_sib_recv, moe_sem.at[n_chip], sibling)
@@ -546,6 +564,9 @@
     tile = 256 if ff % 256 == 0 else ff
     tiles = ff // tile
     top = routes.shape[1]
+    peers = 2 * n_chip
+    capacity = min(n_tok, max(2, n_tok * top * 3 // (4 * peers)))
+    slots = -(-peers * capacity // ROWS) * ROWS
     hbm = pl.BlockSpec(memory_space=pltpu.HBM)
     dma = pltpu.SemaphoreType.DMA
     shapes = (
@@ -569,11 +590,12 @@
         pltpu.VMEM((latents, width), BF16),
         pltpu.VMEM((rows, half), BF16),
         pltpu.VMEM((rows, 128), F32),
-        pltpu.VMEM((tiles, 2, rows, tile), BF16),
-        pltpu.VMEM((tiles, 2, rows, tile), BF16),
-        pltpu.VMEM((tiles, 2, rows, tile), F32),
-        pltpu.VMEM((tiles, rows, tile), BF16),
-        pltpu.VMEM((tiles, rows, tile), BF16),
+        pltpu.VMEM((2, slots, half), BF16),
+        pltpu.VMEM((tiles, 2, slots, tile), BF16),
+        pltpu.VMEM((tiles, 2, slots, tile), BF16),
+        pltpu.VMEM((tiles, 2, slots, tile), F32),
+        pltpu.VMEM((tiles, slots, tile), BF16),
+        pltpu.VMEM((tiles, slots, tile), BF16),
         pltpu.VMEM((side, half), BF16),
         pltpu.VMEM((side, half), BF16),
         pltpu.VMEM((rows, half), F32),

time: 70.6 us -> 68.2 us (0.966)
  Pallas kernels: 69.8 us -> 67.4 us
    pallas_call x1, Pallas kernels: 67.4 us -> 65 us  [local_fused(): pl.pallas_call(functools.partial(layer_kernel, n_tok, n_chip), out_shape=...]
where the time goes in v3:
time: 68.2 us; the launch traced here: 68 us
  Pallas kernels  67.4 us (99%)
    pallas_call x1, Pallas kernels, local_fused(): pl.pallas_call(functools.partial(layer_kernel, n_tok, n_chip), out_shape=...  65 us
    pallas_call x1, Pallas kernels, local_fused(): pl.pallas_call(functools.partial(hand_over, len(shapes)), out_shape=shape...  2.4 us

profile of v3, /device:TPU:0, one launch (start us, length us, event | category | flops | bytes accessed | tf_op | source)
XLA Modules:
  0.0 68.0 jit_solution(8306036675233471701)
XLA Ops:
  0.6 65.0 %shard_map.145 = (bf16[15,1024]{1,0:T(8,128)(2,1)}, bf16[192,2048]{1,0:T(8,128)(2,1)}, bf16[192,2048]{1,0:T(8,128)(2,1)}, f32[1,192]{1,0:T(1,128)}, f32[1,2048]{1,0:T(1,128)}, /*index=5*/f32[1,128]{1,0:T(1,128)}) custom-call(bf16[15,1024]{1,0:T(8,128)(2,1)} %tok_hbm.1, s32[8,15]{1,0:T(8,128)} %bitcast.12, f32[8,15]{1,0:T(8,128)} %bitcast.13, ...), custom_call_target="tpu_custom_call" | custom-call | tf_op jit(solution)/shard_map/pallas_call | solution.py:628
  65.6 2.4 %shard_map.146 = (bf16[15,1024]{1,0:T(8,128)(2,1)}, bf16[192,2048]{1,0:T(8,128)(2,1)}, bf16[192,2048]{1,0:T(8,128)(2,1)}, f32[1,192]{1,0:T(1,128)}, f32[1,2048]{1,0:T(1,128)}, /*index=5*/f32[1,128]{1,0:T(1,128)}) custom-call(bf16[15,1024]{1,0:T(8,128)(2,1)} %get-tuple-element.18.refs_0_, bf16[192,2048]{1,0:T(8,128)(2,1)} %get-tuple-element.19.refs_1_, ...), custom_call_target="tpu_custom_call" | custom-call | tf_op jit(solution)/shard_map/pallas_call | solution.py:649
